TPU v7x, 32 devices: a whole 2x2x4 slice. The times are simulated.
32 devices in a mesh: az: 8 (over z, core), tm: 4 (over y, x).
Axes of the slice: x: 2, y: 2, z: 4, core: 2. Of those that a mesh axis runs over, the one named last changes fastest.
Arguments:
- pressure: bfloat16 [16, 64, 64, 4096], P(None, 'az', 'tm'), may hold values from -6 to 6
- offsets: int32 [64, 16], P('tm'), may hold values from -1 to 0
- frac: float32 [64, 16], P('tm'), may hold values from 0 to 1
Outputs:
- csm: float32 [256, 2, 1024, 1024], P('tm', None, 'az')
All inputs are finite; a program needn't handle non-finite values.
Results may differ from a plain program's by a relative error of at most 0.0065.
Values may be sent and summed in bfloat16 or wider, within the bound.
A program may use at most 256 MiB of HBM per device.

v0:
```python
import math

import jax
import jax.numpy as jnp
from jax import lax
from jax.sharding import PartitionSpec as P

FREQS = 256


def extended(block, sides, width):
    for axis, dim in sides:
        count = lax.axis_size(axis)
        forward = [(i, i + 1) for i in range(count - 1)]
        forward.append((count - 1, 0))
        backward = [(target, source) for source, target in forward]
        low = lax.ppermute(
            lax.slice_in_dim(block, block.shape[dim] - width, None, axis=dim), axis, forward
        )
        high = lax.ppermute(lax.slice_in_dim(block, 0, width, axis=dim), axis, backward)
        block = jnp.concatenate([low, block, high], axis=dim)
    return block


def dft_table(length, freqs):
    times = jnp.arange(length, dtype=jnp.int32)
    bins = jnp.arange(1, freqs + 1, dtype=jnp.int32)
    phase = (times[:, None] * bins[None, :] % length).astype(jnp.float32) * (2.0 * math.pi / length)
    hann = 0.5 - 0.5 * jnp.cos(times.astype(jnp.float32) * (2.0 * math.pi / length))
    factor = hann[:, None] / math.sqrt(3.0 * length / 8.0)
    return jnp.concatenate([factor * jnp.cos(phase), -factor * jnp.sin(phase)], axis=1).astype(
        jnp.bfloat16
    )


def interp_weights(offsets, frac):
    rows = []
    for shift in range(-1, 2):
        low = (offsets == shift).astype(frac.dtype)
        high = (offsets + 1 == shift).astype(frac.dtype)
        rows.append((1.0 - frac) * low + frac * high)
    return jnp.stack(rows, 0)


def rotated_rows(rows):
    split = rows.reshape(rows.shape[0], rows.shape[1], rows.shape[2] // 2, 2)
    return jnp.stack([split[..., 1], -split[..., 0]], -1).reshape(rows.shape)


def cross_terms(rows, turned, columns):
    real = jnp.einsum("fqk,fpk->fqp", rows, columns, preferred_element_type=jnp.float32)
    imag = jnp.einsum("fqk,fpk->fqp", turned, columns, preferred_element_type=jnp.float32)
    return jnp.stack([real, imag], 1)


def shards(pressure, offsets, frac):
    cycles, sector, blocks, length = pressure.shape
    subs = offsets.shape[1]
    sub_len = length // subs
    padded = extended(pressure, (("az", 1),), 1)
    weights = interp_weights(offsets, frac)
    total = jnp.zeros((cycles, sector, blocks, subs, sub_len), jnp.float32)
    for shift in range(3):
        moved = padded[:, shift : shift + sector].reshape(cycles, sector, blocks, subs, sub_len)
        total = total + weights[shift][None, None, :, :, None] * moved
    virtual = total.astype(jnp.bfloat16).reshape(cycles * sector * blocks, length)
    table = dft_table(length, FREQS)
    freqs = table.shape[1] // 2
    spectra = jnp.dot(virtual, table, preferred_element_type=jnp.float32).astype(jnp.bfloat16)
    spectra = spectra.reshape(cycles, sector, blocks, 2, freqs).transpose(4, 1, 0, 2, 3)
    spectra = spectra.reshape(freqs, sector * cycles, blocks, 2)
    local_rows = sector * cycles
    gathered = lax.all_gather(spectra, "az", axis=1, tiled=True)
    shared = lax.all_to_all(gathered, "tm", split_axis=0, concat_axis=2, tiled=True)
    width = shared.shape[2]
    columns = shared.reshape(shared.shape[0], shared.shape[1], width * 2)
    start = lax.axis_index("az") * local_rows
    rows = lax.dynamic_slice_in_dim(columns, start, local_rows, 1)
    result = cross_terms(rows, rotated_rows(rows), columns)
    return result * (1.0 / width)


def solution(mesh):
    return jax.shard_map(
        shards,
        mesh=mesh,
        in_specs=(P(None, "az", "tm", None), P("tm", None), P("tm", None)),
        out_specs=P("tm", None, "az", None),
        check_vma=False,
    )
```

profile of v0, /device:TPU:0, one launch (start us, length us, event | category | flops | bytes accessed | tf_op | source)
XLA Modules:
  0.0 792.2 jit_solution(11718093756187441207)
XLA Ops:
  6.5 2.7 fusion.19
  9.8 4.1 collective-permute-start.1
  13.9 4.8 mul.142
  18.7 36.3 %copy.35 = f32[256,8,16,256]{3,1,2,0:T(8,128)} copy(f32[256,8,16,256]{3,2,1,0:T(8,128)S(1)} %bitcast.38) | data formatting | bytes 67108864
  55.0 4.7 mul.137
  59.8 36.2 %copy.34 = f32[256,8,16,256]{3,1,2,0:T(8,128)} copy(f32[256,8,16,256]{3,2,1,0:T(8,128)S(1)} %bitcast.39) | data formatting | bytes 67108864
  96.0 4.7 mul.132
  100.7 36.4 %copy.33 = f32[256,8,16,256]{3,1,2,0:T(8,128)} copy(f32[256,8,16,256]{3,2,1,0:T(8,128)S(1)} %bitcast.40) | data formatting | bytes 67108864
  137.2 19.0 %multiply_convert_fusion.1 = (bf16[4096,256]{1,0:T(8,128)(2,1)S(1)}, bf16[4096,256]{1,0:T(8,128)(2,1)S(1)}) fusion(s32[256]{0:T(256)S(1)} %iota_add_fusion, f32[4096]{0:T(1024)S(1)} %get-tuple-element.16, f32[4096]{0:T(1024)S(1)} %get-tuple-element.17), kind=kLoop, calls=%fused_computation.22 | loop fusion | flops 18874368 | bytes 4228096 | tf_op jit(solution)/shard_map/convert.3
  156.2 22.6 %pad_maximum_fusion.1 = (bf16[16,8,16,4096]{3,2,1,0:T(8,128)(2,1)}, bf16[16,8,16,4096]{3,2,1,0:T(8,128)(2,1)}) fusion(bf16[16,8,16,4096]{3,2,1,0:T(8,128)(2,1)} %param.3, bf16[16,1,16,4096]{3,2,1,0:T(8,128)(2,1)} %collective-permute-done, bf16[16,1,16,4096]{3,2,1,0:T(8,128)(2,1)} %collective-permute-done.1), kind=kLoop, calls=%fused_computation.8 | loop fusion | flops 16777216 | bytes 54525952 | tf_op jit(solution)/shard_map/concatenate | solution.py:21
  178.8 52.8 %fusion.1 = bf16[2048,4096]{1,0:T(8,128)(2,1)} fusion(f32[2048,4096]{1,0:T(8,128)} %bitcast.35, f32[2048,4096]{1,0:T(8,128)} %bitcast.36, f32[2048,4096]{1,0:T(8,128)} %bitcast.37, bf16[16,8,16,4096]{3,2,1,0:T(8,128)(2,1)} %get-tuple-element.6, bf16[16,8,16,4096]{3,2,1,0:T(8,128)(2,1)} %param.3, bf16[16,8,16,4096]{3,2,1,0:T(8,128)(2,1)} %get-tuple-element.5), kind=kLoop, calls=%fused_computation.3 | loop fusion | flops 75497472 | bytes 167772160 | tf_op jit(solution)/shard_map/convert_element_type | solution.py:66
  231.6 13.3 %fusion.13 = bf16[2048,512]{1,0:T(8,128)(2,1)} fusion(bf16[2048,4096]{1,0:T(8,128)(2,1)} %fusion.1, bf16[4096,256]{1,0:T(8,128)(2,1)S(1)} %get-tuple-element.15, bf16[4096,256]{1,0:T(8,128)(2,1)S(1)} %get-tuple-element.14), kind=kOutput, calls=%fused_computation.26 | convolution fusion | flops 8599371776 | bytes 23068672 | tf_op jit(solution)/shard_map/dot_general | solution.py:69
  245.0 2.5 reshape.53
  249.4 151.2 %all-gather.2.cloned.1.call-done = bf16[256,1024,16,2]{0,2,3,1:T(8,128)(2,1)} async-done(((bf16[256,128,16,2]{0,2,3,1:T(8,128)(2,1)}), bf16[256,1024,16,2]{0,2,3,1:T(8,128)(2,1)}) %all-gather.2.cloned.1.call-update) | async-done | bytes 16777232 | tf_op jit(solution)/shard_map/all_gather | solution.py:73
  400.5 26.0 %copy.25 = bf16[256,1024,16,2]{1,2,3,0:T(8,128)(2,1)} copy(bf16[256,1024,16,2]{0,2,3,1:T(8,128)(2,1)} %all-gather.2.cloned.1.call-done) | data formatting | bytes 33554432 | tf_op jit(solution)/shard_map/all_gather | solution.py:73
  426.5 7.0 all-to-all-start
  433.5 182.9 %all-to-all-done = bf16[256,1024,16,2]{1,2,3,0:T(8,128)(2,1)} async-done(((bf16[256,1024,16,2]{1,2,3,0:T(8,128)(2,1)}), bf16[256,1024,16,2]{1,2,3,0:T(8,128)(2,1)}, u32[]{:S(2)}, u32[]{:S(2)}) %all-to-all-start) | async-done | bytes 16777248 | tf_op jit(solution)/shard_map/all_to_all | solution.py:74
  616.4 18.7 %copy.26 = bf16[64,1024,4,16,2]{1,0,4,3,2:T(8,128)(2,1)} copy(bf16[64,1024,4,16,2]{1,3,4,0,2:T(8,128)(2,1)} %bitcast.6) | data formatting | bytes 33554432 | tf_op jit(solution)/shard_map/all_to_all | solution.py:74
  635.1 22.9 %copy.27 = bf16[64,1024,128]{2,1,0:T(8,128)(2,1)} copy(bf16[64,1024,128]{1,0,2:T(8,128)(2,1)} %bitcast.41) | data formatting | bytes 33554432 | tf_op jit(solution)/shard_map/reshape | solution.py:76
  659.8 2.8 copy.29
  662.5 17.0 %convolution_bitcast_fusion.1 = f32[64,1,128,1024]{3,2,0,1:T(8,128)} fusion(bf16[64,128,128]{2,1,0:T(8,128)(2,1)S(1)} %constant_dynamic-slice_fusion, bf16[64,1024,128]{2,1,0:T(8,128)(2,1)} %copy.27), kind=kOutput, calls=%fused_computation.10 | convolution fusion | flops 2147483648 | bytes 52428800 | tf_op jit(solution)/shard_map/fqk,fpk->fqp/dot_general | solution.py:51
  680.0 17.2 %convolution_bitcast_fusion = f32[64,1,128,1024]{3,2,0,1:T(8,128)} fusion(bf16[64,1024,128]{2,1,0:T(8,128)(2,1)} %copy.27, bf16[64,128,128]{1,0,2:T(8,128)(2,1)S(1)} %bitcast.42), kind=kOutput, calls=%fused_computation.9 | convolution fusion | flops 2147483648 | bytes 52428800 | tf_op jit(solution)/shard_map/fqk,fpk->fqp/dot_general | solution.py:52
  697.1 44.5 %maximum_multiply_fusion = f32[64,2,128,1024]{3,2,0,1:T(8,128)} fusion(f32[64,1,128,1024]{3,2,0,1:T(8,128)} %convolution_bitcast_fusion, f32[64,1,128,1024]{3,2,0,1:T(8,128)} %convolution_bitcast_fusion.1), kind=kLoop, calls=%fused_computation | loop fusion | flops 33554432 | bytes 134217728 | tf_op jit(solution)/shard_map/mul | solution.py:80
  741.6 43.8 %copy.32 = f32[64,2,128,1024]{3,2,1,0:T(8,128)} copy(f32[64,2,128,1024]{3,2,0,1:T(8,128)} %maximum_multiply_fusion) | data formatting | bytes 134217728 | tf_op jit(solution)/shard_map/mul | solution.py:80
  (18 shorter events, 4.6 us)
Async XLA Ops:
  6.5 7.4 copy-start.1
  6.5 7.4 copy-start.2
  6.5 394.0 %all-gather.2.cloned.1.call-start = ((), (), s32[]{:S(2)}) async-start(), calls=%async_computation.1 | async-start | bytes 18874368 | tf_op jit(solution)/shard_map/all_gather | solution.py:73
  9.3 146.9 %collective-permute-start = (bf16[16,1,16,4096]{3,2,1,0:T(8,128)(2,1)S(1)}, bf16[16,1,16,4096]{3,2,1,0:T(8,128)(2,1)}, u32[]{:S(2)}, u32[]{:S(2)}) collective-permute-start(bf16[16,1,16,4096]{3,2,1,0:T(8,128)(2,1)S(1)} %get-tuple-element.7), channel_id=1, source_target_pairs={{0,4},{4,8},{8,12},{12,16},{16,20},{20,24},{24,28},{28,0},{1,5},{5... | collective-permute-start | bytes 6291464 | tf_op jit(solution)/shard_map/ppermute | solution.py:17
  9.8 146.4 %collective-permute-start.1 = (bf16[16,1,16,4096]{3,2,1,0:T(8,128)(2,1)S(1)}, bf16[16,1,16,4096]{3,2,1,0:T(8,128)(2,1)}, u32[]{:S(2)}, u32[]{:S(2)}) collective-permute-start(bf16[16,1,16,4096]{3,2,1,0:T(8,128)(2,1)S(1)} %get-tuple-element.8), channel_id=1, source_target_pairs={{4,0},{8,4},{12,8},{16,12},{20,16},{24,20},{28,24},{0,28},{5,1},{9... | collective-permute-start | bytes 6291464 | tf_op jit(solution)/shard_map/ppermute | solution.py:20
  426.5 189.9 %all-to-all-start = ((bf16[256,1024,16,2]{1,2,3,0:T(8,128)(2,1)}), bf16[256,1024,16,2]{1,2,3,0:T(8,128)(2,1)}, u32[]{:S(2)}, u32[]{:S(2)}) async-start(bf16[256,1024,16,2]{1,2,3,0:T(8,128)(2,1)} %copy.25), calls=%async_computation | async-start | bytes 33554432 | tf_op jit(solution)/shard_map/all_to_all | solution.py:74
  662.5 17.0 %copy-start = (bf16[64,128,128]{1,0,2:T(8,128)(2,1)S(1)}, bf16[64,128,128]{1,0,2:T(8,128)(2,1)}, u32[]{:S(2)}) copy-start(bf16[64,128,128]{1,0,2:T(8,128)(2,1)} %copy.29) | copy-start | bytes 6291460
Sparse Core Ops, SparseCore 0:
  249.5 150.9 all-gather.1
where the time goes:
time: 794 us; the launch traced here: 792 us
  waiting for transfers between devices  334 us (42%)
  local copies, waits for them, and re-layouts  246 us (31%)
  other arithmetic  139 us (18%)
  matrix products  47.5 us (6%)
  between operations  13.5 us (2%)
  starting transfers between devices  11.6 us (1%)
    all_to_all x1, waiting for transfers between devices, shards(): lax.all_to_all(gathered, 'tm', split_axis=0, concat_axis=2, tiled=True)  183 us
    all_gather x1, waiting for transfers between devices, shards(): gathered = lax.all_gather(spectra, 'az', axis=1, tiled=True)  151 us
    unnamed x9, local copies, waits for them, and re-layouts  109 us
    convert_element_type x1, other arithmetic, shards(): total.astype(jnp.bfloat16).reshape(cycles * sector * blocks, length)  52.8 us
    mul x1, other arithmetic, shards(): return result * (1.0 / width)  44.5 us
    mul x1, local copies, waits for them, and re-layouts, shards(): return result * (1.0 / width)  43.8 us
    all_gather x1, local copies, waits for them, and re-layouts, shards(): gathered = lax.all_gather(spectra, 'az', axis=1, tiled=True)  26 us
    reshape x1, local copies, waits for them, and re-layouts, shards(): columns = shared.reshape(shared.shape[0], shared.shape[1], width * 2)  22.9 us
  transfers between devices with their start and end apart: 4, of which 2 were waited for; matrix products, arithmetic and copies ran while one was open for 18% of the time, Pallas kernels for 0%

commit v1 on v0

v1 whole, which is shorter than its diff:
```python
import functools
import math

import jax
import jax.numpy as jnp
import numpy as np
from jax import lax
from jax.experimental import pallas as pl
from jax.experimental.pallas import tpu as pltpu
from jax.sharding import PartitionSpec as P

FREQS = 256
LANES = 128
MIB = 1 << 20


def dft_table(length, freqs):
    times = np.arange(length)
    bins = np.arange(1, freqs + 1)
    phase = (times[:, None] * bins[None, :] % length) * (2.0 * math.pi / length)
    hann = 0.5 - 0.5 * np.cos(times * (2.0 * math.pi / length))
    factor = hann[:, None] / math.sqrt(3.0 * length / 8.0)
    table = np.concatenate([factor * np.cos(phase), -factor * np.sin(phase)], axis=1)
    return jnp.asarray(table.astype(jnp.bfloat16))


def interp_weights(offsets, frac):
    rows = []
    for shift in range(-1, 2):
        low = (offsets == shift).astype(frac.dtype)
        high = (offsets + 1 == shift).astype(frac.dtype)
        rows.append((1.0 - frac) * low + frac * high)
    return jnp.stack(rows, 0)


def spread(weight, sub_len):
    blocks, subs = weight.shape
    parts = [
        jnp.broadcast_to(weight[:, s : s + 1], (blocks, sub_len)) for s in range(subs)
    ]
    return parts


def edge_kernel(w_ref, p_ref, table_ref, out_ref, rows_ref):
    cycles, _, blocks, length = p_ref.shape
    subs = w_ref.shape[2]
    sub_len = length // subs
    weight = w_ref[0]
    for s in range(subs):
        cols = pl.ds(s * sub_len, sub_len)
        wide = jnp.broadcast_to(weight[:, s : s + 1], (blocks, sub_len))
        for r in range(cycles):
            rows_ref[pl.ds(r * blocks, blocks), cols] = (
                wide * p_ref[r, 0, :, cols].astype(jnp.float32)
            ).astype(jnp.bfloat16)
    y = jnp.dot(rows_ref[...], table_ref[...], preferred_element_type=jnp.float32)
    for j in range(out_ref.shape[1]):
        out_ref[0, j] = y[:, j * LANES : (j + 1) * LANES].astype(jnp.bfloat16)


def edge_spectra(weights, pressure, table):
    cycles, sector, blocks, length = pressure.shape
    subs = weights.shape[2]
    width = table.shape[1]
    groups = width // LANES
    rows = cycles * blocks
    return pl.pallas_call(
        edge_kernel,
        grid=(2,),
        in_specs=[
            pl.BlockSpec((1, blocks, subs), lambda i: (2 - 2 * i, 0, 0)),
            pl.BlockSpec((cycles, 1, blocks, length), lambda i: (0, (sector - 1) * i, 0, 0)),
            pl.BlockSpec((length, width), lambda i: (0, 0)),
        ],
        out_specs=pl.BlockSpec((1, groups, rows, LANES), lambda i: (i, 0, 0, 0)),
        out_shape=jax.ShapeDtypeStruct((2, groups, rows, LANES), jnp.bfloat16),
        scratch_shapes=[pltpu.VMEM((rows, length), jnp.bfloat16)],
        compiler_params=pltpu.CompilerParams(vmem_limit_bytes=40 * MIB),
        cost_estimate=pl.CostEstimate(
            flops=4 * rows * length * width, bytes_accessed=9 * MIB, transcendentals=0
        ),
    )(weights, pressure, table)


def main_kernel(w_ref, p_ref, table_ref, out_ref, rows_ref):
    count, sector, blocks, length = p_ref.shape
    subs = w_ref.shape[2]
    sub_len = length // subs
    for s in range(subs):
        cols = pl.ds(s * sub_len, sub_len)
        wide = [
            jnp.broadcast_to(w_ref[j, :, s : s + 1], (blocks, sub_len)) for j in range(3)
        ]
        for r in range(count):
            before = None
            here = p_ref[r, 0, :, cols].astype(jnp.float32)
            for m in range(sector):
                after = None
                total = wide[1] * here
                if m > 0:
                    total = total + wide[0] * before
                if m < sector - 1:
                    after = p_ref[r, m + 1, :, cols].astype(jnp.float32)
                    total = total + wide[2] * after
                rows_ref[pl.ds((m * count + r) * blocks, blocks), cols] = total.astype(
                    jnp.bfloat16
                )
                before, here = here, after
    y = jnp.dot(rows_ref[...], table_ref[...], preferred_element_type=jnp.float32)
    for j in range(out_ref.shape[0]):
        out_ref[j] = y[:, j * LANES : (j + 1) * LANES].reshape(sector, count, blocks, LANES)


def main_spectra(weights, pressure, table):
    cycles, sector, blocks, length = pressure.shape
    subs = weights.shape[2]
    width = table.shape[1]
    groups = width // LANES
    count = 4
    return pl.pallas_call(
        main_kernel,
        grid=(cycles // count,),
        in_specs=[
            pl.BlockSpec((3, blocks, subs), lambda i: (0, 0, 0)),
            pl.BlockSpec((count, sector, blocks, length), lambda i: (i, 0, 0, 0)),
            pl.BlockSpec((length, width), lambda i: (0, 0)),
        ],
        out_specs=pl.BlockSpec(
            (groups, sector, count, blocks, LANES), lambda i: (0, 0, i, 0, 0)
        ),
        out_shape=jax.ShapeDtypeStruct((groups, sector, cycles, blocks, LANES), jnp.float32),
        scratch_shapes=[pltpu.VMEM((count * sector * blocks, length), jnp.bfloat16)],
        compiler_params=pltpu.CompilerParams(vmem_limit_bytes=48 * MIB),
        cost_estimate=pl.CostEstimate(
            flops=2 * cycles * sector * blocks * length * width,
            bytes_accessed=24 * MIB,
            transcendentals=0,
        ),
    )(weights, pressure, table)


def turn_kernel(cycles, blocks, y_ref, low_ref, high_ref, out_ref, edge_ref, turned_ref):
    groups, rows, _ = y_ref.shape
    mics = rows // blocks
    edge_ref[0] = low_ref[0].astype(jnp.float32)
    edge_ref[1] = high_ref[0].astype(jnp.float32)
    for j in range(groups):
        half, place = j // (groups // 2), j % (groups // 2)
        for b in range(blocks):
            piece = y_ref[j, pl.ds(b, mics, stride=blocks), :]
            low = edge_ref[0, j, pl.ds(b, cycles, stride=blocks), :]
            high = edge_ref[1, j, pl.ds(b, cycles, stride=blocks), :]
            piece = jnp.concatenate(
                [
                    piece[:cycles] + low,
                    piece[cycles : mics - cycles],
                    piece[mics - cycles :] + high,
                ],
                0,
            )
            first = place * LANES * 2 * blocks + half * blocks + b
            turned_ref[pl.ds(first, LANES, stride=2 * blocks), :] = piece.T
    out_ref[...] = turned_ref[...].astype(jnp.bfloat16)


def turned_spectra(y, low, high, cycles, blocks):
    groups, rows, _ = y.shape
    mics = rows // blocks
    out_rows = groups * LANES * blocks
    edge_rows = cycles * blocks
    return pl.pallas_call(
        functools.partial(turn_kernel, cycles, blocks),
        in_specs=[
            pl.BlockSpec((groups, rows, LANES), lambda: (0, 0, 0)),
            pl.BlockSpec((1, groups, edge_rows, LANES), lambda: (0, 0, 0, 0)),
            pl.BlockSpec((1, groups, edge_rows, LANES), lambda: (0, 0, 0, 0)),
        ],
        out_specs=pl.BlockSpec((out_rows, mics), lambda: (0, 0)),
        out_shape=jax.ShapeDtypeStruct((out_rows, mics), jnp.bfloat16),
        scratch_shapes=[
            pltpu.VMEM((2, groups, edge_rows, LANES), jnp.float32),
            pltpu.VMEM((out_rows, mics), jnp.float32),
        ],
        compiler_params=pltpu.CompilerParams(vmem_limit_bytes=40 * MIB),
    )(y, low, high)


def cross_kernel(blocks, own_ref, all_ref, out_ref):
    count = own_ref.shape[0]
    sectors, _, depth, mics = all_ref.shape
    scale = 1.0 / (depth // 2)
    part = depth // 2 // (depth // (2 * blocks))
    for i in range(count):
        rows = own_ref[i].astype(jnp.float32)
        pieces = []
        for k in range(0, depth, 2 * part):
            pieces.append(rows[k + part : k + 2 * part])
            pieces.append(-rows[k : k + part])
        turned = jnp.concatenate(pieces, 0)
        left = jnp.concatenate([rows.T, turned.T], 0).astype(jnp.bfloat16)
        for a in range(sectors):
            res = jnp.dot(left, all_ref[a, i], preferred_element_type=jnp.float32) * scale
            cols = pl.ds(a * mics, mics)
            out_ref[i, 0, :, cols] = res[:mics]
            out_ref[i, 1, :, cols] = res[mics:]


def cross_spectra(own, every, blocks):
    freqs, depth, mics = own.shape
    sectors = every.shape[0]
    count = 4
    return pl.pallas_call(
        functools.partial(cross_kernel, blocks),
        grid=(freqs // count,),
        in_specs=[
            pl.BlockSpec((count, depth, mics), lambda i: (i, 0, 0)),
            pl.BlockSpec((sectors, count, depth, mics), lambda i: (0, i, 0, 0)),
        ],
        out_specs=pl.BlockSpec((count, 2, mics, sectors * mics), lambda i: (i, 0, 0, 0)),
        out_shape=jax.ShapeDtypeStruct((freqs, 2, mics, sectors * mics), jnp.float32),
        compiler_params=pltpu.CompilerParams(vmem_limit_bytes=40 * MIB),
    )(own, every)


def shards(pressure, offsets, frac):
    cycles, sector, blocks, length = pressure.shape
    table = dft_table(length, FREQS)
    weights = interp_weights(offsets, frac)
    count = lax.axis_size("az")
    forward = [(i, (i + 1) % count) for i in range(count)]
    backward = [(target, source) for source, target in forward]
    edges = edge_spectra(weights, pressure, table)
    high = lax.ppermute(edges[0:1], "az", backward)
    low = lax.ppermute(edges[1:2], "az", forward)
    y = main_spectra(weights, pressure, table)
    y = y.reshape(y.shape[0], sector * cycles * blocks, LANES)
    spectra = turned_spectra(y, low, high, cycles, blocks)
    spectra = spectra.reshape(FREQS, 2 * blocks, sector * cycles)
    own = lax.all_to_all(spectra, "tm", split_axis=0, concat_axis=1, tiled=True)
    every = lax.all_gather(own, "az", axis=0, tiled=False)
    return cross_spectra(own, every, blocks)


def solution(mesh):
    return jax.shard_map(
        shards,
        mesh=mesh,
        in_specs=(P(None, "az", "tm", None), P("tm", None), P("tm", None)),
        out_specs=P("tm", None, "az", None),
        check_vma=False,
    )
```

time: 794 us -> 254 us (0.32)
  local copies, waits for them, and re-layouts: 246 us -> 5.78 us
  waiting for transfers between devices: 334 us -> 150 us
  other arithmetic: 139 us -> 0.73 us
  Pallas kernels: 0 us -> 50.2 us
  matrix products: 47.5 us -> 0 us
  blocking collectives: 0 us -> 27.8 us
    all_to_all x1 -> x0, waiting for transfers between devices: 183 us -> none  [shards(): lax.all_to_all(gathered, 'tm', split_axis=0, concat_axis=2, tiled=True)]
    unnamed x9 -> x4, local copies, waits for them, and re-layouts: 109 us -> 3.77 us
    mul x4 -> x0, local copies, waits for them, and re-layouts: 58 us -> none  [the longest x1 43.8 us: shards(): return result * (1.0 / width)]
    convert_element_type x1 -> x0, other arithmetic: 52.8 us -> none  [shards(): total.astype(jnp.bfloat16).reshape(cycles * sector * blocks, length)]
    pallas_call x0 -> x4, Pallas kernels: none -> 50.2 us  [the longest x1 28.4 us: cross_spectra(): pl.pallas_call(functools.partial(cross_kernel, blocks), grid=(freqs // co...]
    dot_general x3 -> x0, matrix products: 47.5 us -> none  [the longest x1 17.2 us: cross_terms(): jnp.einsum('fqk,fpk->fqp', turned, columns, preferred_element_type=jnp.fl...]
    mul x1 -> x0, other arithmetic: 44.5 us -> none  [shards(): return result * (1.0 / width)]
    all_to_all x0 -> x1, blocking collectives: none -> 27.8 us  [shards(): own = lax.all_to_all(spectra, 'tm', split_axis=0, concat_axis=1, tiled=True)]
  transfers between devices with their start and end apart: 4 -> 3, of which waited for: 2 -> 1; matrix products, arithmetic and copies ran while one was open for 18% -> 0% of each run, Pallas kernels for 0% -> 5%
where the time goes in v1:
time: 254 us; the launch traced here: 253 us
  waiting for transfers between devices  150 us (59%)
  Pallas kernels  50.2 us (20%)
  blocking collectives  27.8 us (11%)
  between operations  13.4 us (5%)
  local copies, waits for them, and re-layouts  5.78 us (2%)
  starting transfers between devices  4.55 us (2%)
    all_gather x1, waiting for transfers between devices, shards(): every = lax.all_gather(own, 'az', axis=0, tiled=False)  150 us
    pallas_call x1, Pallas kernels, cross_spectra(): pl.pallas_call(functools.partial(cross_kernel, blocks), grid=(freqs // co...  28.4 us
    all_to_all x1, blocking collectives, shards(): own = lax.all_to_all(spectra, 'tm', split_axis=0, concat_axis=1, tiled=True)  27.8 us
    pallas_call x1, Pallas kernels, main_spectra(): pl.pallas_call(main_kernel, grid=(cycles // count,), in_specs=[pl.BlockSp...  13.3 us
  transfers between devices with their start and end apart: 3, of which 1 were waited for; matrix products, arithmetic and copies ran while one was open for 0% of the time, Pallas kernels for 5%

profile of v1, /device:TPU:0, one launch (start us, length us, event | category | flops | bytes accessed | tf_op | source)
XLA Modules:
  0.0 252.9 jit_solution(5297962887130757693)
XLA Ops:
  6.5 0.0 all-gather.2.cloned.1.call-start
  6.5 0.7 add_bitcast_fusion.2
  7.3 0.0 copy-start.1
  7.3 2.2 copy-done.1
  9.5 4.2 %shard_map.47 = bf16[2,4,256,128]{3,2,1,0:T(8,128)(2,1)S(1)} custom-call(f32[3,16,16]{2,1,0:T(8,128)S(1)} %pad_maximum_fusion.w_ref, bf16[16,8,16,4096]{3,2,1,0:T(8,128)(2,1)} %p_ref.3, bf16[4096,512]{1,0:T(8,128)(2,1)S(1)} %copy-done.1), custom_call_target="tpu_custom_call" | custom-call | flops 2147483648 | bytes 9437184 | tf_op jit(solution)/shard_map/pallas_call | solution.py:67
  13.7 4.5 %collective-permute-start.1 = (bf16[1,4,256,128]{3,2,1,0:T(8,128)(2,1)S(1)}, bf16[1,4,256,128]{3,2,1,0:T(8,128)(2,1)S(1)}, u32[]{:S(2)}, u32[]{:S(2)}) collective-permute-start(bf16[1,4,256,128]{3,2,1,0:T(8,128)(2,1)S(1)} %get-tuple-element.5), channel_id=1, source_target_pairs={{4,0},{8,4},{12,8},{16,12},{20,16},{24,20},{28,24},{0,28},{5,1},{9... | collective-permute-start | bytes 786440 | tf_op jit(solution)/shard_map/ppermute | solution.py:233
  18.3 0.0 collective-permute-start
  18.3 13.3 %shard_map.46 = f32[4,8,16,16,128]{4,3,2,1,0:T(8,128)S(1)} custom-call(f32[3,16,16]{2,1,0:T(8,128)S(1)} %pad_maximum_fusion.w_ref, bf16[16,8,16,4096]{3,2,1,0:T(8,128)(2,1)} %p_ref.3, bf16[4096,512]{1,0:T(8,128)(2,1)} %constant.17.clone.table_ref), custom_call_target="tpu_custom_call" | custom-call | flops 8589934592 | bytes 25165824 | tf_op jit(solution)/shard_map/pallas_call | solution.py:120
  31.6 0.0 collective-permute-done.1.high_ref
  31.6 0.0 collective-permute-done.low_ref
  31.6 4.2 %shard_map.48 = bf16[8192,128]{1,0:T(8,128)(2,1)S(1)} custom-call(f32[4,2048,128]{2,1,0:T(8,128)S(1)} %bitcast.16, bf16[1,4,256,128]{3,2,1,0:T(8,128)(2,1)S(1)} %collective-permute-done.low_ref, bf16[1,4,256,128]{3,2,1,0:T(8,128)(2,1)S(1)} %collective-permute-done.1.high_ref), custom_call_target="tpu_custom_call" | custom-call | tf_op jit(solution)/shard_map/pallas_call | solution.py:171
  35.9 27.8 %all_to_all.18 = bf16[256,32,128]{2,1,0:T(8,128)(2,1)S(1)} all-to-all(bf16[256,32,128]{2,1,0:T(8,128)(2,1)S(1)} %bitcast.15), channel_id=1, replica_groups=mesh['az'=8,'tm'=4] {'tm'}, dimensions={0} | all-to-all | bytes 4194304 | tf_op jit(solution)/shard_map/all_to_all | solution.py:239
  63.6 2.0 copy.8
  65.6 0.0 all-gather.2.cloned.1.call-update
  65.6 150.5 %all-gather.2.cloned.1.call-done.all_ref = bf16[8,64,128,128]{3,2,1,0:T(8,128)(2,1)} async-done(((bf16[1,64,128,128]{3,2,1,0:T(8,128)(2,1)}), bf16[8,64,128,128]{3,2,1,0:T(8,128)(2,1)}) %all-gather.2.cloned.1.call-update) | async-done | bytes 16777232 | tf_op jit(solution)/shard_map/all_gather | solution.py:240
  216.1 0.0 copy-start
  216.1 1.6 copy-done
  217.7 28.4 %shard_map.49 = f32[64,2,128,1024]{3,2,1,0:T(8,128)} custom-call(bf16[64,128,128]{2,1,0:T(8,128)(2,1)S(1)} %bitcast.14, bf16[8,64,128,128]{3,2,1,0:T(8,128)(2,1)} %all-gather.2.cloned.1.call-done.all_ref), custom_call_target="tpu_custom_call" | custom-call | tf_op jit(solution)/shard_map/pallas_call | solution.py:212
  (2 shorter events, 0.0 us)
Async XLA Ops:
  6.5 209.6 %all-gather.2.cloned.1.call-start = ((), (), s32[]{:S(2)}) async-start(), calls=%async_computation.1 | async-start | bytes 18874368 | tf_op jit(solution)/shard_map/all_gather | solution.py:240
  7.3 2.2 copy-start.1
  13.7 17.9 %collective-permute-start.1 = (bf16[1,4,256,128]{3,2,1,0:T(8,128)(2,1)S(1)}, bf16[1,4,256,128]{3,2,1,0:T(8,128)(2,1)S(1)}, u32[]{:S(2)}, u32[]{:S(2)}) collective-permute-start(bf16[1,4,256,128]{3,2,1,0:T(8,128)(2,1)S(1)} %get-tuple-element.5), channel_id=1, source_target_pairs={{4,0},{8,4},{12,8},{16,12},{20,16},{24,20},{28,24},{0,28},{5,1},{9... | collective-permute-start | bytes 786440 | tf_op jit(solution)/shard_map/ppermute | solution.py:233
  18.3 13.4 %collective-permute-start = (bf16[1,4,256,128]{3,2,1,0:T(8,128)(2,1)S(1)}, bf16[1,4,256,128]{3,2,1,0:T(8,128)(2,1)S(1)}, u32[]{:S(2)}, u32[]{:S(2)}) collective-permute-start(bf16[1,4,256,128]{3,2,1,0:T(8,128)(2,1)S(1)} %get-tuple-element.6), channel_id=1, source_target_pairs={{0,4},{4,8},{8,12},{12,16},{16,20},{20,24},{24,28},{28,0},{1,5},{5... | collective-permute-start | bytes 786440 | tf_op jit(solution)/shard_map/ppermute | solution.py:234
  216.1 1.6 copy-start
Sparse Core Ops, SparseCore 0:
  65.8 150.2 all-gather.1

commit v2 on v1

--- a/solution.py
+++ b/solution.py
@@ -10,6 +10,7 @@
 from jax.sharding import PartitionSpec as P
 
 FREQS = 256
+EIGHTHS = (1, 6, 1)
 LANES = 128
 MIB = 1 << 20
 
@@ -139,7 +140,8 @@
     )(weights, pressure, table)
 
 
-def turn_kernel(cycles, blocks, y_ref, low_ref, high_ref, out_ref, edge_ref, turned_ref):
+def turn_kernel(cycles, blocks, y_ref, low_ref, high_ref, *refs):
+    outs, (edge_ref, turned_ref) = refs[:-2], refs[-2:]
     groups, rows, _ = y_ref.shape
     mics = rows // blocks
     edge_ref[0] = low_ref[0].astype(jnp.float32)
@@ -160,14 +162,20 @@
             )
             first = place * LANES * 2 * blocks + half * blocks + b
             turned_ref[pl.ds(first, LANES, stride=2 * blocks), :] = piece.T
-    out_ref[...] = turned_ref[...].astype(jnp.bfloat16)
-
-
-def turned_spectra(y, low, high, cycles, blocks):
+    first = 0
+    for i in range(outs[0].shape[0]):
+        for out_ref in outs:
+            count = out_ref.shape[1]
+            out_ref[i] = turned_ref[pl.ds(first, count), :].astype(jnp.bfloat16)
+            first += count
+
+
+def turned_spectra(y, low, high, cycles, blocks, places):
     groups, rows, _ = y.shape
     mics = rows // blocks
     out_rows = groups * LANES * blocks
     edge_rows = cycles * blocks
+    pieces = [(places, out_rows // places * part // 8, mics) for part in EIGHTHS]
     return pl.pallas_call(
         functools.partial(turn_kernel, cycles, blocks),
         in_specs=[
@@ -175,8 +183,8 @@
             pl.BlockSpec((1, groups, edge_rows, LANES), lambda: (0, 0, 0, 0)),
             pl.BlockSpec((1, groups, edge_rows, LANES), lambda: (0, 0, 0, 0)),
         ],
-        out_specs=pl.BlockSpec((out_rows, mics), lambda: (0, 0)),
-        out_shape=jax.ShapeDtypeStruct((out_rows, mics), jnp.bfloat16),
+        out_specs=[pl.BlockSpec(piece, lambda: (0, 0, 0)) for piece in pieces],
+        out_shape=[jax.ShapeDtypeStruct(piece, jnp.bfloat16) for piece in pieces],
         scratch_shapes=[
             pltpu.VMEM((2, groups, edge_rows, LANES), jnp.float32),
             pltpu.VMEM((out_rows, mics), jnp.float32),
@@ -185,7 +193,8 @@
     )(y, low, high)
 
 
-def cross_kernel(blocks, own_ref, all_ref, out_ref):
+def cross_kernel(blocks, own_ref, all_ref, *refs):
+    out_ref = refs[-1]
     count = own_ref.shape[0]
     sectors, _, depth, mics = all_ref.shape
     scale = 1.0 / (depth // 2)
@@ -205,21 +214,33 @@
             out_ref[i, 1, :, cols] = res[mics:]
 
 
-def cross_spectra(own, every, blocks):
+def cross_spectra(own, every, blocks, first, total, partial):
     freqs, depth, mics = own.shape
     sectors = every.shape[0]
     count = 4
+    skip = first // count
+    shape = (total, 2, mics, sectors * mics)
+    before = [] if partial is None else [partial]
     return pl.pallas_call(
         functools.partial(cross_kernel, blocks),
         grid=(freqs // count,),
         in_specs=[
             pl.BlockSpec((count, depth, mics), lambda i: (i, 0, 0)),
             pl.BlockSpec((sectors, count, depth, mics), lambda i: (0, i, 0, 0)),
-        ],
-        out_specs=pl.BlockSpec((count, 2, mics, sectors * mics), lambda i: (i, 0, 0, 0)),
-        out_shape=jax.ShapeDtypeStruct((freqs, 2, mics, sectors * mics), jnp.float32),
+        ]
+        + [pl.BlockSpec(memory_space=pl.ANY)] * len(before),
+        out_specs=pl.BlockSpec(
+            (count, 2, mics, sectors * mics), lambda i: (skip + i, 0, 0, 0)
+        ),
+        out_shape=jax.ShapeDtypeStruct(shape, jnp.float32),
+        input_output_aliases={2: 0} if before else {},
         compiler_params=pltpu.CompilerParams(vmem_limit_bytes=40 * MIB),
-    )(own, every)
+        cost_estimate=pl.CostEstimate(
+            flops=4 * freqs * depth * mics * mics * sectors,
+            bytes_accessed=8 * freqs * mics * mics * sectors,
+            transcendentals=0,
+        ),
+    )(own, every, *before)
 
 
 def shards(pressure, offsets, frac):
@@ -234,11 +255,19 @@
     low = lax.ppermute(edges[1:2], "az", forward)
     y = main_spectra(weights, pressure, table)
     y = y.reshape(y.shape[0], sector * cycles * blocks, LANES)
-    spectra = turned_spectra(y, low, high, cycles, blocks)
-    spectra = spectra.reshape(FREQS, 2 * blocks, sector * cycles)
-    own = lax.all_to_all(spectra, "tm", split_axis=0, concat_axis=1, tiled=True)
-    every = lax.all_gather(own, "az", axis=0, tiled=False)
-    return cross_spectra(own, every, blocks)
+    places = lax.axis_size("tm")
+    pieces = turned_spectra(y, low, high, cycles, blocks, places)
+    owned, gathered = [], []
+    for piece in pieces:
+        piece = piece.reshape(-1, 2 * blocks, sector * cycles)
+        own = lax.all_to_all(piece, "tm", split_axis=0, concat_axis=1, tiled=True)
+        owned.append(own)
+        gathered.append(lax.all_gather(own, "az", axis=0, tiled=False))
+    result, first = None, 0
+    for own, every in zip(owned, gathered):
+        result = cross_spectra(own, every, blocks, first, FREQS // places, result)
+        first += own.shape[0]
+    return result
 
 
 def solution(mesh):

time: 254 us -> 233 us (0.917)
  waiting for transfers between devices: 150 us -> 115 us
  blocking collectives: 27.8 us -> 37.3 us
  local copies, waits for them, and re-layouts: 5.78 us -> 13 us
    all_gather x1 -> x3, waiting for transfers between devices: 150 us -> 115 us  [shards(): gathered.append(lax.all_gather(own, 'az', axis=0, tiled=False))]
    all_to_all x1 -> x3, blocking collectives: 27.8 us -> 37.3 us  [shards(): own = lax.all_to_all(piece, 'tm', split_axis=0, concat_axis=1, tiled=True)]
    unnamed x4 -> x14, local copies, waits for them, and re-layouts: 3.77 us -> 9.95 us
    pallas_call x1 -> x3, Pallas kernels: 28.4 us -> 27.1 us  [cross_spectra(): pl.pallas_call(functools.partial(cross_kernel, blocks), grid=(freqs // co...]
  transfers between devices with their start and end apart: 3 -> 5, of which waited for: 1 -> 2; matrix products, arithmetic and copies ran while one was open for 0% -> 1% of each run, Pallas kernels for 5% -> 16%
where the time goes in v2:
time: 233 us
  waiting for transfers between devices  115 us (49%)
  Pallas kernels  48.9 us (21%)
  blocking collectives  37.3 us (16%)
  between operations  13.2 us (6%)
  local copies, waits for them, and re-layouts  13 us (6%)
  starting transfers between devices  4.7 us (2%)
    all_gather x3, waiting for transfers between devices, shards(): gathered.append(lax.all_gather(own, 'az', axis=0, tiled=False))  115 us
    all_to_all x3, blocking collectives, shards(): own = lax.all_to_all(piece, 'tm', split_axis=0, concat_axis=1, tiled=True)  37.3 us
    pallas_call x3, Pallas kernels, cross_spectra(): pl.pallas_call(functools.partial(cross_kernel, blocks), grid=(freqs // co...  27.1 us
    pallas_call x1, Pallas kernels, main_spectra(): pl.pallas_call(main_kernel, grid=(cycles // count,), in_specs=[pl.BlockSp...  13.3 us
    unnamed x14, local copies, waits for them, and re-layouts  9.95 us
  transfers between devices with their start and end apart: 5, of which 2 were waited for; matrix products, arithmetic and copies ran while one was open for 1% of the time, Pallas kernels for 16%

profile of v2, /device:TPU:0, one launch (start us, length us, event | category | flops | bytes accessed | tf_op | source)
XLA Modules:
  0.0 232.9 jit_solution(181300634567978919)
XLA Ops:
  6.5 0.7 add_bitcast_fusion.2
  7.3 2.2 copy-done.2
  9.5 4.2 %shard_map.47 = bf16[2,4,256,128]{3,2,1,0:T(8,128)(2,1)S(1)} custom-call(f32[3,16,16]{2,1,0:T(8,128)S(1)} %pad_maximum_fusion.w_ref, bf16[16,8,16,4096]{3,2,1,0:T(8,128)(2,1)} %p_ref.3, bf16[4096,512]{1,0:T(8,128)(2,1)S(1)} %copy-done.2), custom_call_target="tpu_custom_call" | custom-call | flops 2147483648 | bytes 9437184 | tf_op jit(solution)/shard_map/pallas_call | solution.py:68
  13.7 0.5 collective-permute-start
  14.2 4.1 %collective-permute-start.1 = (bf16[1,4,256,128]{3,2,1,0:T(8,128)(2,1)S(1)}, bf16[1,4,256,128]{3,2,1,0:T(8,128)(2,1)S(1)}, u32[]{:S(2)}, u32[]{:S(2)}) collective-permute-start(bf16[1,4,256,128]{3,2,1,0:T(8,128)(2,1)S(1)} %get-tuple-element.11), channel_id=1, source_target_pairs={{4,0},{8,4},{12,8},{16,12},{20,16},{24,20},{28,24},{0,28},{5,1},{9... | collective-permute-start | bytes 786440 | tf_op jit(solution)/shard_map/ppermute | solution.py:254
  18.3 13.3 %shard_map.46 = f32[4,8,16,16,128]{4,3,2,1,0:T(8,128)S(1)} custom-call(f32[3,16,16]{2,1,0:T(8,128)S(1)} %pad_maximum_fusion.w_ref, bf16[16,8,16,4096]{3,2,1,0:T(8,128)(2,1)} %p_ref.3, bf16[4096,512]{1,0:T(8,128)(2,1)} %constant.17.clone.table_ref), custom_call_target="tpu_custom_call" | custom-call | flops 8589934592 | bytes 25165824 | tf_op jit(solution)/shard_map/pallas_call | solution.py:121
  31.7 4.2 %shard_map.48 = (bf16[4,256,128]{2,1,0:T(8,128)(2,1)S(1)}, bf16[4,1536,128]{2,1,0:T(8,128)(2,1)S(1)}, bf16[4,256,128]{2,1,0:T(8,128)(2,1)S(1)}) custom-call(f32[4,2048,128]{2,1,0:T(8,128)S(1)} %bitcast.27, bf16[1,4,256,128]{3,2,1,0:T(8,128)(2,1)S(1)} %collective-permute-done.low_ref, bf16[1,4,256,128]{3,2,1,0:T(8,128)(2,1)S(1)} %collective-permute-done.1.high_ref), custom_call_target="tpu_custom_call" | custom-call | tf_op jit(solution)/shard_map/pallas_call | solution.py:179
  35.9 9.7 %all_to_all.54 = bf16[32,32,128]{2,1,0:T(8,128)(2,1)S(1)} all-to-all(bf16[32,32,128]{2,1,0:T(8,128)(2,1)S(1)} %bitcast.34), channel_id=1, replica_groups=mesh['az'=8,'tm'=4] {'tm'}, dimensions={0} | all-to-all | bytes 524288 | tf_op jit(solution)/shard_map/all_to_all | solution.py:263
  45.6 0.7 copy.20
  46.4 0.0 all-gather.6.cloned.1.call-start
  46.4 19.5 %all_to_all.55 = bf16[192,32,128]{2,1,0:T(8,128)(2,1)S(1)} all-to-all(bf16[192,32,128]{2,1,0:T(8,128)(2,1)S(1)} %bitcast.32), channel_id=1, replica_groups=mesh['az'=8,'tm'=4] {'tm'}, dimensions={0} | all-to-all | bytes 3145728 | tf_op jit(solution)/shard_map/all_to_all | solution.py:263
  65.9 1.6 copy.18
  67.6 0.0 all-gather.4.cloned.1.call-start
  67.6 8.1 %all_to_all.56 = bf16[32,32,128]{2,1,0:T(8,128)(2,1)S(1)} all-to-all(bf16[32,32,128]{2,1,0:T(8,128)(2,1)S(1)} %bitcast.33), channel_id=1, replica_groups=mesh['az'=8,'tm'=4] {'tm'}, dimensions={0} | all-to-all | bytes 524288 | tf_op jit(solution)/shard_map/all_to_all | solution.py:263
  75.7 0.7 copy.16
  76.5 0.0 all-gather.8.cloned.1.call-done.all_ref
  76.5 1.6 copy-done.6
  78.1 4.3 %shard_map.49.refs_0_ = f32[64,2,128,1024]{3,2,1,0:T(8,128)} custom-call(bf16[8,128,128]{2,1,0:T(8,128)(2,1)S(1)} %bitcast.29, bf16[8,8,128,128]{3,2,1,0:T(8,128)(2,1)S(1)} %copy-done.6), custom_call_target="tpu_custom_call" | custom-call | flops 536870912 | bytes 8388608 | tf_op jit(solution)/shard_map/pallas_call | solution.py:224
  82.4 109.0 %all-gather.6.cloned.1.call-done.all_ref = bf16[8,48,128,128]{3,2,1,0:T(8,128)(2,1)} async-done(((bf16[1,48,128,128]{3,2,1,0:T(8,128)(2,1)}), bf16[8,48,128,128]{3,2,1,0:T(8,128)(2,1)}) %all-gather.6.cloned.1.call-update) | async-done | bytes 12582928 | tf_op jit(solution)/shard_map/all_gather | solution.py:265
  191.4 4.6 %copy-done.1 = bf16[8,48,128,128]{3,2,1,0:T(8,128)(2,1)S(1)} copy-done((bf16[8,48,128,128]{3,2,1,0:T(8,128)(2,1)S(1)}, bf16[8,48,128,128]{3,2,1,0:T(8,128)(2,1)}, u32[]{:S(2)}) %copy-start.1) | copy-done | bytes 12582936
  196.0 18.5 %shard_map.50.refs_0_ = f32[64,2,128,1024]{3,2,1,0:T(8,128)} custom-call(bf16[48,128,128]{2,1,0:T(8,128)(2,1)S(1)} %bitcast.26, bf16[8,48,128,128]{3,2,1,0:T(8,128)(2,1)S(1)} %copy-done.1, f32[64,2,128,1024]{3,2,1,0:T(8,128)} %shard_map.49.refs_0_), custom_call_target="tpu_custom_call", output_to_operand_aliasing={{}: (2, {})} | custom-call | flops 3221225472 | bytes 50331648 | tf_op jit(solution)/shard_map/pallas_call | solution.py:224
  214.5 5.9 %all-gather.4.cloned.1.call-done.all_ref = bf16[8,8,128,128]{3,2,1,0:T(8,128)(2,1)} async-done(((bf16[1,8,128,128]{3,2,1,0:T(8,128)(2,1)}), bf16[8,8,128,128]{3,2,1,0:T(8,128)(2,1)}) %all-gather.4.cloned.1.call-update) | async-done | bytes 2097168 | tf_op jit(solution)/shard_map/all_gather | solution.py:265
  220.4 1.6 copy-done.5
  222.0 4.3 %shard_map.51 = f32[64,2,128,1024]{3,2,1,0:T(8,128)} custom-call(bf16[8,128,128]{2,1,0:T(8,128)(2,1)S(1)} %bitcast.31, bf16[8,8,128,128]{3,2,1,0:T(8,128)(2,1)S(1)} %copy-done.5, f32[64,2,128,1024]{3,2,1,0:T(8,128)} %shard_map.50.refs_0_), custom_call_target="tpu_custom_call", output_to_operand_aliasing={{}: (2, {})} | custom-call | flops 536870912 | bytes 8388608 | tf_op jit(solution)/shard_map/pallas_call | solution.py:224
  (18 shorter events, 0.1 us)
Async XLA Ops:
  6.5 70.0 %all-gather.8.cloned.1.call-start = ((), (), s32[]{:S(2)}) async-start(), calls=%async_computation.5 | async-start | bytes 2359296 | tf_op jit(solution)/shard_map/all_gather | solution.py:265
  7.3 2.2 copy-start.2
  13.7 18.0 %collective-permute-start = (bf16[1,4,256,128]{3,2,1,0:T(8,128)(2,1)S(1)}, bf16[1,4,256,128]{3,2,1,0:T(8,128)(2,1)S(1)}, u32[]{:S(2)}, u32[]{:S(2)}) collective-permute-start(bf16[1,4,256,128]{3,2,1,0:T(8,128)(2,1)S(1)} %get-tuple-element.12), channel_id=1, source_target_pairs={{0,4},{4,8},{8,12},{12,16},{16,20},{20,24},{24,28},{28,0},{1,5},{5... | collective-permute-start | bytes 786440 | tf_op jit(solution)/shard_map/ppermute | solution.py:255
  14.2 17.5 %collective-permute-start.1 = (bf16[1,4,256,128]{3,2,1,0:T(8,128)(2,1)S(1)}, bf16[1,4,256,128]{3,2,1,0:T(8,128)(2,1)S(1)}, u32[]{:S(2)}, u32[]{:S(2)}) collective-permute-start(bf16[1,4,256,128]{3,2,1,0:T(8,128)(2,1)S(1)} %get-tuple-element.11), channel_id=1, source_target_pairs={{4,0},{8,4},{12,8},{16,12},{20,16},{24,20},{28,24},{0,28},{5,1},{9... | collective-permute-start | bytes 786440 | tf_op jit(solution)/shard_map/ppermute | solution.py:254
  46.4 145.1 %all-gather.6.cloned.1.call-start = ((), (), s32[]{:S(2)}) async-start(), calls=%async_computation.4 | async-start | bytes 14155776 | tf_op jit(solution)/shard_map/all_gather | solution.py:265
  46.4 30.1 %copy-start.3 = (bf16[8,4,32,128]{3,2,1,0:T(8,128)(2,1)S(1)}, bf16[8,4,32,128]{3,2,1,0:T(8,128)(2,1)}, u32[]{:S(2)}) copy-start(bf16[8,4,32,128]{3,2,1,0:T(8,128)(2,1)} %copy.20) | copy-start | bytes 786436
  67.6 152.8 %all-gather.4.cloned.1.call-start = ((), (), s32[]{:S(2)}) async-start(), calls=%async_computation.3 | async-start | bytes 2359296 | tf_op jit(solution)/shard_map/all_gather | solution.py:265
  76.5 1.6 copy-start.6
  78.1 113.3 %copy-start = (bf16[48,4,32,128]{3,2,1,0:T(8,128)(2,1)S(1)}, bf16[48,4,32,128]{3,2,1,0:T(8,128)(2,1)}, u32[]{:S(2)}) copy-start(bf16[48,4,32,128]{3,2,1,0:T(8,128)(2,1)} %copy.18) | copy-start | bytes 4718596
  191.4 4.6 %copy-start.1 = (bf16[8,48,128,128]{3,2,1,0:T(8,128)(2,1)S(1)}, bf16[8,48,128,128]{3,2,1,0:T(8,128)(2,1)}, u32[]{:S(2)}) copy-start(bf16[8,48,128,128]{3,2,1,0:T(8,128)(2,1)} %all-gather.6.cloned.1.call-done.all_ref) | copy-start | bytes 37748740
  196.0 24.4 %copy-start.4 = (bf16[8,4,32,128]{3,2,1,0:T(8,128)(2,1)S(1)}, bf16[8,4,32,128]{3,2,1,0:T(8,128)(2,1)}, u32[]{:S(2)}) copy-start(bf16[8,4,32,128]{3,2,1,0:T(8,128)(2,1)} %copy.16) | copy-start | bytes 786436
  220.4 1.6 copy-start.5
Sparse Core Ops, SparseCore 0:
  46.5 27.0 all-gather.7
  75.2 116.2 all-gather.5
  193.0 27.3 all-gather.3
